TPU v7x, 128 devices: a whole 4x4x4 slice. The times are simulated.
128 devices in a mesh: row: 16 (over z_lo, y, core), col: 8 (over z_hi, x).
Axes of the slice: x: 4, y: 4, z: 4 (z_hi: 2, z_lo: 2; z = z_hi * 2 + z_lo), core: 2. Of those that a mesh axis runs over, the one named last changes fastest.
Arguments:
- teacher: bfloat16 [24576, 512], P(('row', 'col')), may hold values from -2.5 to 2.5
- student: bfloat16 [24576, 512], P(('row', 'col')), may hold values from -2.5 to 2.5
Outputs:
- grad_student: float32 [24576, 512], P(('row', 'col'))
All inputs are finite; a program needn't handle non-finite values.
Results may differ from a plain program's by a relative error of at most 0.0017.
Values may be sent and summed in bfloat16 or wider, within the bound.
A program may use at most 64 MiB of HBM per device.

v0:
```python
import math

import jax
import jax.numpy as jnp
from jax import lax
from jax.sharding import PartitionSpec as P


def scores_pair(block_t, block_s, cols_t, cols_s, first, row_pos, col_pos, shard, scale):
    dims = (((1,), (1,)), ((), ()))
    zt = lax.dot_general(block_t, cols_t, dims, preferred_element_type=jnp.float32) * scale
    zs = lax.dot_general(block_s, cols_s, dims, preferred_element_type=jnp.float32) * scale
    across = first + jnp.arange(block_t.shape[0], dtype=jnp.int32)
    down = jnp.arange(cols_t.shape[0], dtype=jnp.int32)
    self_pair = (
        ((across // shard)[:, None] == row_pos)
        & ((down // shard)[None, :] == col_pos)
        & ((across % shard)[:, None] == (down % shard)[None, :])
    )
    return (jnp.where(self_pair, -1e30, zt), jnp.where(self_pair, -1e30, zs))


def flatten(value):
    return value.reshape((-1,) + value.shape[2:])


def over_blocks(work, arrays, shard):
    total = arrays[0].shape[0]
    width = shard
    while width < 512 and width < total:
        width = width * 2
    count = total // width
    starts = jnp.arange(count, dtype=jnp.int32) * width
    stacked = tuple((item.reshape((count, width) + item.shape[1:]) for item in arrays))

    def step(pair):
        return work(pair[0], pair[1])

    return lax.map(step, (starts, stacked))


def build_tiles(rows_t, rows_s, cols_t, cols_s, row_pos, col_pos, shard, scale, reduce_stats):

    def first_pass(first, blocks):
        zt, zs = scores_pair(
            blocks[0], blocks[1], cols_t, cols_s, first, row_pos, col_pos, shard, scale
        )
        top_t = jnp.max(zt, axis=1)
        top_s = jnp.max(zs, axis=1)
        return (
            top_t,
            jnp.sum(jnp.exp(zt - top_t[:, None]), axis=1),
            top_s,
            jnp.sum(jnp.exp(zs - top_s[:, None]), axis=1),
        )

    local = tuple((flatten(item) for item in over_blocks(first_pass, (rows_t, rows_s), shard)))
    stats = reduce_stats(local)

    def second_pass(first, blocks):
        zt, zs = scores_pair(
            blocks[0], blocks[1], cols_t, cols_s, first, row_pos, col_pos, shard, scale
        )
        teach = jnp.exp(zt - blocks[2][:, None]) / blocks[3][:, None]
        learn = jnp.exp(zs - blocks[4][:, None]) / blocks[5][:, None]
        return (learn - teach).astype(jnp.bfloat16)

    return flatten(over_blocks(second_pass, (rows_t, rows_s) + tuple(stats), shard))


def left_term(gtile, cols_s):
    return jnp.dot(gtile, cols_s, preferred_element_type=jnp.float32)


def right_term(gtile, rows_s):
    return lax.dot_general(
        gtile, rows_s, (((0,), (0,)), ((), ())), preferred_element_type=jnp.float32
    )


def on_device(teacher, student):
    shard = teacher.shape[0]
    scale = 1.0 / (0.1 * math.sqrt(teacher.shape[1]))
    row_index = lax.axis_index("row")
    col_index = lax.axis_index("col")
    rows_t, rows_s = (
        lax.all_gather(teacher, "col", axis=0, tiled=True),
        lax.all_gather(student, "col", axis=0, tiled=True),
    )
    cols_t, cols_s = (
        lax.all_gather(teacher, "row", axis=0, tiled=True),
        lax.all_gather(student, "row", axis=0, tiled=True),
    )

    def reduce_stats(local):
        top_t, top_s = lax.pmax((local[0], local[2]), "col")
        totals = lax.psum(
            (local[1] * jnp.exp(local[0] - top_t), local[3] * jnp.exp(local[2] - top_s)), "col"
        )
        return (top_t, totals[0], top_s, totals[1])

    gtile = build_tiles(
        rows_t, rows_s, cols_t, cols_s, col_index, row_index, shard, scale, reduce_stats
    )
    forward = lax.psum_scatter(left_term(gtile, cols_s), "col", scatter_dimension=0, tiled=True)
    backward = lax.psum_scatter(right_term(gtile, rows_s), "row", scatter_dimension=0, tiled=True)
    return scale * (forward + backward)


def solution(mesh):
    return jax.shard_map(
        on_device,
        mesh=mesh,
        in_specs=(P(("row", "col"), None), P(("row", "col"), None)),
        out_specs=P(("row", "col"), None),
        check_vma=False,
    )
```

profile of v0, /device:TPU:0, one launch (start us, length us, event | category | flops | bytes accessed | tf_op | source)
XLA Modules:
  0.0 508.5 jit_solution(12610157627418316113)
XLA Ops:
  6.5 0.7 all-gather.5.cloned.1.call-update
  9.4 54.0 %all-gather.5.cloned.1.call-done = bf16[1536,512]{1,0:T(8,128)(2,1)} async-done(((bf16[192,512]{1,0:T(8,128)(2,1)}), bf16[1536,512]{1,0:T(8,128)(2,1)}) %all-gather.5.cloned.1.call-update) | async-done | bytes 1572880 | tf_op jit(solution)/shard_map/all_gather | solution.py:88
  63.4 52.2 %all-gather.9.cloned.1.call-done = bf16[1536,512]{1,0:T(8,128)(2,1)} async-done(((bf16[192,512]{1,0:T(8,128)(2,1)}), bf16[1536,512]{1,0:T(8,128)(2,1)}) %all-gather.9.cloned.1.call-update) | async-done | bytes 1572880 | tf_op jit(solution)/shard_map/all_gather | solution.py:87
  115.6 36.1 %all-gather.7.cloned.1.call-done = bf16[3072,512]{1,0:T(8,128)(2,1)} async-done(((bf16[192,512]{1,0:T(8,128)(2,1)}), bf16[3072,512]{1,0:T(8,128)(2,1)}) %all-gather.7.cloned.1.call-update) | async-done | bytes 3145744 | tf_op jit(solution)/shard_map/all_gather | solution.py:92
  151.8 37.6 %all-gather.11.cloned.1.call-done = bf16[3072,512]{1,0:T(8,128)(2,1)} async-done(((bf16[192,512]{1,0:T(8,128)(2,1)}), bf16[3072,512]{1,0:T(8,128)(2,1)}) %all-gather.11.cloned.1.call-update) | async-done | bytes 3145744 | tf_op jit(solution)/shard_map/all_gather | solution.py:91
  189.3 38.8 %while.32 = (s32[]{:T(128)}, f32[2,768]{1,0:T(2,128)S(1)}, f32[2,768]{1,0:T(2,128)S(1)}, f32[2,768]{1,0:T(2,128)S(1)}, f32[2,768]{1,0:T(2,128)S(1)}, /*index=5*/...) while((s32[]{:T(128)}, f32[2,768]{1,0:T(2,128)S(1)}, ...), condition=%wide.region_5.6_spmd, body=%wide.region_0.5_spmd.sunk | while | flops 4879079936 | bytes 74051816 | solution.py:39
  190.0 1.0 fusion.76
  191.0 4.8 fusion.77
  195.8 0.7 add_select_fusion.8
  196.6 5.2 %fusion.78 = (f32[768]{0:T(1024)S(1)}, f32[768]{0:T(1024)S(1)}, f32[768,3072]{1,0:T(8,128)S(1)}) fusion(s32[3072]{0:T(1024)S(1)} %fusion.74, s32[768]{0:T(1024)S(1)} %add_select_fusion.8, pred[3072]{0:T(1024)(128)(4,1)S(1)} %fusion.75, pred[768]{0:T(1024)(128)(4,1)S(1)} %fusion.76, f32[768,3072]{1,0:T(8,128)S(1)} %fusion.77, ...), kind=kOutput, calls=%fused_computation.6.clone.1 | convolution fusion | flops 2437151232 | bytes 22833156 | tf_op jit(solution)/shard_map/while/body/eval_jaxpr/dot_general | solution.py:12
  201.7 6.7 %exponential_reduce_fusion.3 = (f32[768]{0:T(1024)S(1)}, f32[768]{0:T(1024)S(1)}) fusion(f32[768,3072]{1,0:T(8,128)S(1)} %get-tuple-element.617, f32[768]{0:T(1024)S(1)} %get-tuple-element.618, s32[3072]{0:T(1024)S(1)} %fusion.74, s32[768]{0:T(1024)S(1)} %add_select_fusion.8, pred[3072]{0:T(1024)(128)(4,1)S(1)} %fusion.75, ...), kind=kLoop, calls=%fused_computation.clone.1 | loop fusion | flops 25950720 | bytes 18905856 | tf_op jit(solution)/shard_map/while/body/eval_jaxpr/reduce_sum | solution.py:54
  209.4 1.0 fusion.76
  210.4 4.8 fusion.77
  215.2 0.7 add_select_fusion.8
  216.0 5.2 %fusion.78 = (f32[768]{0:T(1024)S(1)}, f32[768]{0:T(1024)S(1)}, f32[768,3072]{1,0:T(8,128)S(1)}) fusion(s32[3072]{0:T(1024)S(1)} %fusion.74, s32[768]{0:T(1024)S(1)} %add_select_fusion.8, pred[3072]{0:T(1024)(128)(4,1)S(1)} %fusion.75, pred[768]{0:T(1024)(128)(4,1)S(1)} %fusion.76, f32[768,3072]{1,0:T(8,128)S(1)} %fusion.77, ...), kind=kOutput, calls=%fused_computation.6.clone.1 | convolution fusion | flops 2437151232 | bytes 22833156 | tf_op jit(solution)/shard_map/while/body/eval_jaxpr/dot_general | solution.py:12
  221.2 6.7 %exponential_reduce_fusion.3 = (f32[768]{0:T(1024)S(1)}, f32[768]{0:T(1024)S(1)}) fusion(f32[768,3072]{1,0:T(8,128)S(1)} %get-tuple-element.617, f32[768]{0:T(1024)S(1)} %get-tuple-element.618, s32[3072]{0:T(1024)S(1)} %fusion.74, s32[768]{0:T(1024)S(1)} %add_select_fusion.8, pred[3072]{0:T(1024)(128)(4,1)S(1)} %fusion.75, ...), kind=kLoop, calls=%fused_computation.clone.1 | loop fusion | flops 25950720 | bytes 18905856 | tf_op jit(solution)/shard_map/while/body/eval_jaxpr/reduce_sum | solution.py:54
  228.2 41.7 %all-reduce.1 = (f32[1536]{0:T(1024)S(1)}, f32[1536]{0:T(1024)S(1)}) all-reduce(f32[1536]{0:T(1024)S(1)} %reshape.139, f32[1536]{0:T(1024)S(1)} %reshape.143), channel_id=1, replica_groups=mesh['row'=16,'col'=8] {'col'}, use_global_device_ids=true, to_apply=%region_8.9 | all-reduce | flops 3072 | bytes 24576 | tf_op jit(solution)/shard_map/pmax | solution.py:96
  269.9 36.8 %all-reduce = (f32[2,768]{1,0:T(2,128)S(1)}, f32[2,768]{1,0:T(2,128)S(1)}) all-reduce(f32[2,768]{1,0:T(2,128)S(1)} %reshape.142, f32[2,768]{1,0:T(2,128)S(1)} %reshape.146), channel_id=1, replica_groups=mesh['row'=16,'col'=8] {'col'}, use_global_device_ids=true, to_apply=%region_9.10 | all-reduce | flops 3072 | bytes 24576 | tf_op jit(solution)/shard_map/psum | solution.py:97
  306.8 34.0 %while.33 = (s32[]{:T(128)}, bf16[2,768,3072]{2,1,0:T(8,128)(2,1)}, s32[2]{0:T(128)S(1)}, s32[]{:T(128)}, s32[]{:T(128)}, /*index=5*/bf16[2,768,512]{2,1,0:T(8,1...) while((s32[]{:T(128)}, bf16[2,768,3072]{2,1,0:T(8,128)(2,1)}, ...), condition=%wide.region_11.12_spmd, body=%wide.region_10.11_spmd.sunk | while | flops 4862568448 | bytes 50414048 | solution.py:39
  307.5 1.1 fusion.86
  308.6 4.8 fusion.83
  313.4 0.7 add_select_fusion.9
  314.1 9.6 %bitcast_dynamic-update-slice_fusion.2 = bf16[2,768,3072]{2,1,0:T(8,128)(2,1)} fusion(bf16[2,768,3072]{2,1,0:T(8,128)(2,1)} %get-tuple-element.695, s32[]{:T(128)} %get-tuple-element.694, f32[768]{0:T(1024)S(1)} %get-tuple-element.634, f32[768]{0:T(1024)S(1)} %get-tuple-element.635, bf16[3072,512]{1,0:T(8,128)(2,1)S(1)} %copy-done.1, ...), kind=kOutput, calls=%fused_computation.38.clone.1 | convolution fusion | flops 2446589952 | bytes 18125824 | tf_op jit(solution)/shard_map/while/body/eval_jaxpr/dot_general | solution.py:11
  324.5 1.1 fusion.86
  325.5 4.8 fusion.83
  330.3 0.7 add_select_fusion.9
  331.1 9.7 %bitcast_dynamic-update-slice_fusion.2 = bf16[2,768,3072]{2,1,0:T(8,128)(2,1)} fusion(bf16[2,768,3072]{2,1,0:T(8,128)(2,1)} %get-tuple-element.695, s32[]{:T(128)} %get-tuple-element.694, f32[768]{0:T(1024)S(1)} %get-tuple-element.634, f32[768]{0:T(1024)S(1)} %get-tuple-element.635, bf16[3072,512]{1,0:T(8,128)(2,1)S(1)} %copy-done.1, ...), kind=kOutput, calls=%fused_computation.38.clone.1 | convolution fusion | flops 2446589952 | bytes 18125824 | tf_op jit(solution)/shard_map/while/body/eval_jaxpr/dot_general | solution.py:11
  340.8 10.8 %fusion.45 = f32[1536,512]{1,0:T(8,128)} fusion(bf16[1536,3072]{1,0:T(8,128)(2,1)} %bitcast.54, bf16[3072,512]{1,0:T(8,128)(2,1)} %get-tuple-element.744), kind=kOutput, calls=%fused_computation.76 | convolution fusion | flops 4831838208 | bytes 15728640 | tf_op jit(solution)/shard_map/dot_general | solution.py:72
  351.7 11.0 %fusion.46 = f32[3072,512]{1,0:T(8,128)} fusion(bf16[1536,3072]{1,0:T(8,128)(2,1)} %bitcast.55, bf16[1536,512]{1,0:T(8,128)(2,1)S(1)} %bitcast.52), kind=kOutput, calls=%fused_computation.77 | convolution fusion | flops 4831838208 | bytes 17301504 | tf_op jit(solution)/shard_map/dot_general | solution.py:76
  362.7 65.2 %reduce-scatter.3.cloned.1.call-done = f32[192,512]{1,0:T(8,128)} async-done(((f32[1536,512]{1,0:T(8,128)}), f32[192,512]{1,0:T(8,128)}) %reduce-scatter.3.cloned.1.call-update) | async-done | bytes 393232 | tf_op jit(solution)/shard_map/reduce_scatter | solution.py:105
  427.9 71.8 %reduce-scatter.5.cloned.1.call-done = f32[192,512]{1,0:T(8,128)} async-done(((f32[3072,512]{1,0:T(8,128)}), f32[192,512]{1,0:T(8,128)}) %reduce-scatter.5.cloned.1.call-update) | async-done | bytes 393232 | tf_op jit(solution)/shard_map/reduce_scatter | solution.py:106
  499.7 1.9 add_multiply_fusion
  (76 shorter events, 5.5 us)
Async XLA Ops:
  6.5 56.9 %all-gather.5.cloned.1.call-start = ((), (), s32[]{:S(2)}) async-start(), calls=%async_computation.2 | async-start | bytes 1769472 | tf_op jit(solution)/shard_map/all_gather | solution.py:88
  7.3 108.4 %all-gather.9.cloned.1.call-start = ((), (), s32[]{:S(2)}) async-start(), calls=%async_computation.4 | async-start | bytes 1769472 | tf_op jit(solution)/shard_map/all_gather | solution.py:87
  8.0 143.7 %all-gather.7.cloned.1.call-start = ((), (), s32[]{:S(2)}) async-start(), calls=%async_computation.3 | async-start | bytes 3342336 | tf_op jit(solution)/shard_map/all_gather | solution.py:92
  8.7 180.6 %all-gather.11.cloned.1.call-start = ((), (), s32[]{:S(2)}) async-start(), calls=%async_computation.5 | async-start | bytes 3342336 | tf_op jit(solution)/shard_map/all_gather | solution.py:91
  9.3 418.6 %reduce-scatter.3.cloned.1.call-start = ((), (), s32[]{:S(2)}) async-start(), calls=%async_computation.6 | async-start | bytes 3538944 | tf_op jit(solution)/shard_map/reduce_scatter | solution.py:105
  189.3 7.2 %copy-start = (bf16[3072,512]{1,0:T(8,128)(2,1)S(1)}, bf16[3072,512]{1,0:T(8,128)(2,1)}, u32[]{:S(2)}) copy-start(bf16[3072,512]{1,0:T(8,128)(2,1)} %get-tuple-element.677) | copy-start | bytes 9437188 | tf_op jit(solution)/shard_map/while
  189.3 7.2 %copy-start.2 = (bf16[2,768,512]{2,1,0:T(8,128)(2,1)S(1)}, bf16[2,768,512]{2,1,0:T(8,128)(2,1)}, u32[]{:S(2)}) copy-start(bf16[2,768,512]{2,1,0:T(8,128)(2,1)} %get-tuple-element.676) | copy-start | bytes 4718596 | tf_op jit(solution)/shard_map/while
  208.7 7.3 %copy-start = (bf16[3072,512]{1,0:T(8,128)(2,1)S(1)}, bf16[3072,512]{1,0:T(8,128)(2,1)}, u32[]{:S(2)}) copy-start(bf16[3072,512]{1,0:T(8,128)(2,1)} %get-tuple-element.677) | copy-start | bytes 9437188 | tf_op jit(solution)/shard_map/while
  208.7 7.3 %copy-start.2 = (bf16[2,768,512]{2,1,0:T(8,128)(2,1)S(1)}, bf16[2,768,512]{2,1,0:T(8,128)(2,1)}, u32[]{:S(2)}) copy-start(bf16[2,768,512]{2,1,0:T(8,128)(2,1)} %get-tuple-element.676) | copy-start | bytes 4718596 | tf_op jit(solution)/shard_map/while
  306.8 7.3 %copy-start.1 = (bf16[3072,512]{1,0:T(8,128)(2,1)S(1)}, bf16[3072,512]{1,0:T(8,128)(2,1)}, u32[]{:S(2)}) copy-start(bf16[3072,512]{1,0:T(8,128)(2,1)} %get-tuple-element.718) | copy-start | bytes 9437188 | tf_op jit(solution)/shard_map/while
  306.8 7.3 %copy-start.4 = (bf16[2,768,512]{2,1,0:T(8,128)(2,1)S(1)}, bf16[2,768,512]{2,1,0:T(8,128)(2,1)}, u32[]{:S(2)}) copy-start(bf16[2,768,512]{2,1,0:T(8,128)(2,1)} %get-tuple-element.717) | copy-start | bytes 4718596 | tf_op jit(solution)/shard_map/while
  323.7 7.3 %copy-start.1 = (bf16[3072,512]{1,0:T(8,128)(2,1)S(1)}, bf16[3072,512]{1,0:T(8,128)(2,1)}, u32[]{:S(2)}) copy-start(bf16[3072,512]{1,0:T(8,128)(2,1)} %get-tuple-element.718) | copy-start | bytes 9437188 | tf_op jit(solution)/shard_map/while
  323.7 7.3 %copy-start.4 = (bf16[2,768,512]{2,1,0:T(8,128)(2,1)S(1)}, bf16[2,768,512]{2,1,0:T(8,128)(2,1)}, u32[]{:S(2)}) copy-start(bf16[2,768,512]{2,1,0:T(8,128)(2,1)} %get-tuple-element.717) | copy-start | bytes 4718596 | tf_op jit(solution)/shard_map/while
  340.8 10.9 %copy-start.3 = (bf16[2,768,512]{2,1,0:T(8,128)(2,1)S(1)}, bf16[2,768,512]{2,1,0:T(8,128)(2,1)}, u32[]{:S(2)}) copy-start(bf16[2,768,512]{2,1,0:T(8,128)(2,1)} %get-tuple-element.749) | copy-start | bytes 4718596
  351.6 148.1 %reduce-scatter.5.cloned.1.call-start = ((), (), s32[]{:S(2)}) async-start(), calls=%async_computation.7 | async-start | bytes 6684672 | tf_op jit(solution)/shard_map/reduce_scatter | solution.py:106
Sparse Core Ops, SparseCore 0:
  9.7 53.7 all-gather.4
  65.7 49.8 all-gather.8
  117.3 34.3 all-gather.6
  153.3 35.9 all-gather.10
  351.7 76.1 reduce-scatter.2
  430.3 69.3 reduce-scatter.4
where the time goes:
time: 509 us; the launch traced here: 508 us
  waiting for transfers between devices  320 us (63%)
  blocking collectives  78.5 us (15%)
  matrix products  70.5 us (14%)
  other arithmetic  22.5 us (4%)
  between operations  13.6 us (3%)
    reduce_scatter x1, waiting for transfers between devices, on_device(): lax.psum_scatter(right_term(gtile, rows_s), 'row', scatter_dimension=0, t...  71.8 us
    reduce_scatter x1, waiting for transfers between devices, on_device(): lax.psum_scatter(left_term(gtile, cols_s), 'col', scatter_dimension=0, ti...  65.2 us
    all_gather x1, waiting for transfers between devices, on_device(): lax.all_gather(student, 'col', axis=0, tiled=True)  54 us
    all_gather x1, waiting for transfers between devices, on_device(): lax.all_gather(teacher, 'col', axis=0, tiled=True)  52.2 us
    pmax x1, blocking collectives, reduce_stats(): top_t, top_s = lax.pmax((local[0], local[2]), 'col')  41.7 us
    all_gather x1, waiting for transfers between devices, on_device(): lax.all_gather(teacher, 'row', axis=0, tiled=True)  37.6 us
    psum x1, blocking collectives, reduce_stats(): lax.psum((local[1] * jnp.exp(local[0] - top_t), local[3] * jnp.exp(local[...  36.8 us
    all_gather x1, waiting for transfers between devices, on_device(): lax.all_gather(student, 'row', axis=0, tiled=True)  36.1 us
  transfers between devices with their start and end apart: 6, of which 6 were waited for; matrix products, arithmetic and copies ran while one was open for 2% of the time, Pallas kernels for 0%

commit v1 on v0

v1 whole, which is shorter than its diff:
```python
import math

import jax
import jax.numpy as jnp
from jax import lax
from jax.experimental import pallas as pl
from jax.experimental.pallas import tpu as pltpu
from jax.sharding import PartitionSpec as P

F32 = jnp.float32
BF16 = jnp.bfloat16
MESH = pl.DeviceIdType.MESH
SIDE = 4

OFFSETS = (
    (0, 0, 0), (3, 0, 0), (0, 0, 1), (1, 0, 0), (0, 3, 3), (3, 1, 0),
    (1, 0, 1), (0, 2, 3), (3, 2, 0), (3, 1, 3), (1, 0, 2),
)
PARENT = (None, 0, 0, 0, 0, 1, 2, 4, 5, 5, 6)
SLOTS = len(OFFSETS)
CHILDREN = tuple(tuple(q for q in range(SLOTS) if PARENT[q] == p) for p in range(SLOTS))
ARRIVALS = (
    (0, 0), (0, 1), (2, 0), (1, 0), (4, 0), (3, 0), (2, 1), (1, 1), (4, 1), (3, 1),
    (6, 0), (5, 0), (7, 0), (6, 1), (5, 1), (7, 1), (10, 0), (8, 0), (9, 0), (10, 1), (8, 1), (9, 1),
)


def minus(a, b):
    return tuple((p - q) % SIDE for p, q in zip(a, b))


def work_lists():
    found, pairs = set(), [(0, 0, 1)]
    for j in range(SLOTS):
        for i in range(j):
            d = minus(OFFSETS[j], OFFSETS[i])
            e = minus((0, 0, 0), d)
            if min(d, e) not in found:
                found.add(min(d, e))
                pairs.append((i, j, int(d == e)))
    assert len(found) == (SIDE**3 - 1 + 7) // 2
    cores = ([], [])
    for kind in (0, 1):
        for n, pair in enumerate(p for p in pairs if p[2] == kind):
            cores[(n + kind) % 2].append(pair)
    return tuple(sorted(c, key=lambda p: (max(p[:2]), p)) for c in cores)


WORK = work_lists()
STEPS = len(WORK[0])


def last_slot(n):
    return max(max(WORK[core][m][:2]) for core in (0, 1) for m in range(n + 1))


def first_use(q):
    return min(n for core in (0, 1) for n in range(STEPS) if q in WORK[core][n][:2])


def table(core, n, field):
    value = jnp.int32(0)
    for m in range(STEPS):
        one, two = WORK[0][m][field], WORK[1][m][field]
        if one == two:
            entry = jnp.int32(one)
        else:
            entry = jnp.where(core == 0, jnp.int32(one), jnp.int32(two))
        value = jnp.where(n == m, entry, value)
    return value


def kernel(
    t_ref, s_ref, o_ref, rows, z, acc, stat, stat_in, both, both_in, norm, half_in, part_in,
    tree_send, tree_recv, pair_send, pair_recv, stat_send, stat_recv, both_send, both_recv,
    norm_send, norm_recv, half_send, half_recv, part_send, part_recv,
):
    shard, width = t_ref.shape
    full = 2 * shard
    scale = 1.0 / (0.1 * math.sqrt(width))
    row = lax.axis_index("row")
    col = lax.axis_index("col")
    core = lax.rem(row, 2)
    other = 1 - core
    y = lax.rem(lax.div(row, 2), SIDE)
    x = lax.rem(col, SIDE)
    zz = lax.div(col, SIDE) * 2 + lax.div(row, 2 * SIDE)

    def device(d, to_core, sign=1):
        at = [lax.rem(p + (sign * q) % SIDE, SIDE) for p, q in zip((x, y, zz), d)]
        return (
            (lax.rem(at[2], 2) * SIDE + at[1]) * 2 + to_core,
            lax.div(at[2], 2) * SIDE + at[0],
        )

    sibling = (lax.div(row, 2) * 2 + other, col)

    def edge(q):
        return minus(OFFSETS[q], OFFSETS[PARENT[q]])

    partners = set()
    for q in range(1, SLOTS):
        for d in (OFFSETS[q], edge(q)):
            partners.add(d)
            partners.add(minus((0, 0, 0), d))
    partners = sorted(partners)

    barrier = pltpu.get_barrier_semaphore()
    for d in partners:
        pl.semaphore_signal(barrier, inc=1, device_id=device(d, core), device_id_type=MESH)
    pl.semaphore_signal(barrier, inc=1, device_id=sibling, device_id_type=MESH)
    rows[0, 0, core] = t_ref[...]
    rows[0, 1, core] = s_ref[...]
    pl.semaphore_wait(barrier, len(partners) + 1)

    def remote(src, dst, send, recv, to):
        return pltpu.make_async_remote_copy(
            src_ref=src, dst_ref=dst, send_sem=send, recv_sem=recv, device_id=to, device_id_type=MESH
        )

    def tree(q, m):
        return remote(
            rows.at[PARENT[q], m, core], rows.at[q, m, core], tree_send.at[q, m], tree_recv.at[q, m],
            device(edge(q), core, -1),
        )

    def across(q, m):
        return remote(
            rows.at[q, m, core], rows.at[q, m, core], pair_send.at[q, m], pair_recv.at[q, m], sibling
        )

    def take_up(q, m):
        if q:
            tree(q, m).wait_recv()
        for child in CHILDREN[q]:
            tree(child, m).start()
        across(q, m).start()

    for q, m in ARRIVALS[:2]:
        take_up(q, m)

    acc[...] = jnp.zeros_like(acc)
    for m in range(2):
        stat[:, 2 * m : 2 * m + 1, :] = jnp.full((SLOTS, 1, full), -1e30, F32)
        stat[:, 2 * m + 1 : 2 * m + 2, :] = jnp.zeros((SLOTS, 1, full), F32)

    def block(q, m):
        return rows[q, m].reshape(full, width)

    def as_row(column):
        return jnp.transpose(jnp.broadcast_to(column, (full, 128)))[0:1]

    def as_column(line):
        wide = jnp.transpose(jnp.broadcast_to(line, (128, full)))
        return jnp.concatenate([wide] * (full // 128), axis=1)

    def merge(ref, m, top, total):
        old = ref[2 * m : 2 * m + 1, :]
        new = jnp.maximum(old, top)
        ref[2 * m + 1 : 2 * m + 2, :] = ref[2 * m + 1 : 2 * m + 2, :] * jnp.exp2(
            old - new
        ) + total * jnp.exp2(top - new)
        ref[2 * m : 2 * m + 1, :] = new

    def first_pass(n, _):
        for q in range(SLOTS):
            @pl.when(n == first_use(q))
            def _(q=q):
                for p, m in ARRIVALS[2:]:
                    if taken_at[p] == first_use(q) and owner_of[p] == q:
                        take_up(p, m)
                for m in range(2):
                    across(q, m).wait_recv()

        a, b = table(core, n, 0), table(core, n, 1)
        weight = jnp.where(table(core, n, 2) == 1, F32(0.5), F32(1.0))
        for m in range(2):
            z[n, m] = lax.dot_general(
                block(a, m), block(b, m), (((1,), (1,)), ((), ())), preferred_element_type=F32
            ) * (scale * math.log2(math.e))

        @pl.when(a == b)
        def _():
            own = lax.broadcasted_iota(jnp.int32, (full, full), 0) == lax.broadcasted_iota(
                jnp.int32, (full, full), 1
            )
            for m in range(2):
                z[n, m] = jnp.where(own, -1e30, z[n, m])

        for m in range(2):
            score = z[n, m]
            right = jnp.max(score, axis=1, keepdims=True)
            down = jnp.max(score, axis=0, keepdims=True)
            right_sum = jnp.sum(jnp.exp2(score - right), axis=1, keepdims=True)
            down_sum = jnp.sum(jnp.exp2(score - down), axis=0, keepdims=True)
            merge(stat.at[a], m, as_row(right), weight * as_row(right_sum))
            merge(stat.at[b], m, down, weight * down_sum)
        return 0

    level = {0: 0}
    for q in range(1, SLOTS):
        level[q] = level[PARENT[q]] + 1
    taken_at, owner_of = {}, {}
    for q in range(1, SLOTS):
        peers = [p for p in range(SLOTS) if level[p] == level[q]]
        head = min(peers, key=lambda p: (first_use(p), p))
        taken_at[q], owner_of[q] = first_use(head), head

    lax.fori_loop(0, STEPS, first_pass, 0)

    def stat_copy(q):
        return remote(
            stat.at[q], stat_in.at[q], stat_send.at[q], stat_recv.at[q], device(OFFSETS[q], core)
        )

    def norm_copy(q):
        return remote(
            norm.at[0], norm.at[q], norm_send.at[q], norm_recv.at[q], device(OFFSETS[q], core, -1)
        )

    for q in range(1, SLOTS):
        stat_copy(q).start()
    both[...] = stat[0]
    for q in range(1, SLOTS):
        stat_copy(q).wait_recv()
        for m in range(2):
            merge(both, m, stat_in[q, 2 * m : 2 * m + 1, :], stat_in[q, 2 * m + 1 : 2 * m + 2, :])
    both_copy = remote(both, both_in, both_send, both_recv, sibling)
    both_copy.start()
    both_copy.wait()
    for m in range(2):
        merge(both, m, both_in[2 * m : 2 * m + 1, :], both_in[2 * m + 1 : 2 * m + 2, :])
    for m in range(2):
        norm[0, m : m + 1, :] = both[2 * m : 2 * m + 1, :] + jnp.log2(both[2 * m + 1 : 2 * m + 2, :])
    for q in range(1, SLOTS):
        norm_copy(q).start()
    for q in range(1, SLOTS):
        norm_copy(q).wait_recv()

    def half_copy(q):
        return remote(
            acc.at[q, other], half_in.at[q], half_send.at[q], half_recv.at[q], sibling
        )

    def part_copy(q):
        return remote(
            acc.at[q, core], part_in.at[q], part_send.at[q], part_recv.at[q], device(edge(q), core)
        )

    def pass_on(q):
        half_copy(q).wait_recv()
        total = acc[q, core] + half_in[q]
        for child in CHILDREN[q]:
            part_copy(child).wait_recv()
            total = total + part_in[child]
        if q:
            acc[q, core] = total
            part_copy(q).start()
        else:
            o_ref[...] = scale * total

    done = {
        q: max(STEPS - 1 - n for core_ in (0, 1) for n in range(STEPS) if q in WORK[core_][n][:2])
        for q in range(SLOTS)
    }

    def second_pass(step, _):
        n = STEPS - 1 - step
        a, b = table(core, n, 0), table(core, n, 1)
        less = table(core, n, 2).astype(F32)
        left = [as_column(norm[a, m : m + 1, :] + less) for m in range(2)]
        top = [norm[b, m : m + 1, :] + less for m in range(2)]
        zt, zs = z[n, 0], z[n, 1]
        by_row = (jnp.exp2(zs - left[1]) - jnp.exp2(zt - left[0])).astype(BF16)
        by_col = (jnp.exp2(zs - top[1]) - jnp.exp2(zt - top[0])).astype(BF16)
        sa, sb = block(a, 1), block(b, 1)
        forward = jnp.dot(by_row, sb, preferred_element_type=F32) + jnp.dot(
            by_col, sb, preferred_element_type=F32
        )
        acc[a] = acc[a] + forward.reshape(2, shard, width)
        dims = (((0,), (0,)), ((), ()))
        backward = lax.dot_general(by_row, sa, dims, preferred_element_type=F32) + lax.dot_general(
            by_col, sa, dims, preferred_element_type=F32
        )
        acc[b] = acc[b] + backward.reshape(2, shard, width)
        for q in reversed(range(SLOTS)):
            @pl.when(step == done[q])
            def _(q=q):
                half_copy(q).start()
        return 0

    lax.fori_loop(0, STEPS, second_pass, 0)
    for q in reversed(range(SLOTS)):
        pass_on(q)

    for q in range(SLOTS):
        for m in range(2):
            if q:
                tree(q, m).wait_send()
            across(q, m).wait_send()
        half_copy(q).wait_send()
        if q:
            stat_copy(q).wait_send()
            norm_copy(q).wait_send()
            part_copy(q).wait_send()


def on_device(teacher, student):
    shard, width = teacher.shape
    full = 2 * shard
    dma = pltpu.SemaphoreType.DMA
    return pl.pallas_call(
        kernel,
        out_shape=jax.ShapeDtypeStruct((shard, width), F32),
        in_specs=[pl.BlockSpec(memory_space=pltpu.VMEM)] * 2,
        out_specs=pl.BlockSpec(memory_space=pltpu.VMEM),
        scratch_shapes=[
            pltpu.VMEM((SLOTS, 2, 2, shard, width), BF16),
            pltpu.VMEM((STEPS, 2, full, full), F32),
            pltpu.VMEM((SLOTS, 2, shard, width), F32),
            pltpu.VMEM((SLOTS, 8, full), F32),
            pltpu.VMEM((SLOTS, 8, full), F32),
            pltpu.VMEM((8, full), F32),
            pltpu.VMEM((8, full), F32),
            pltpu.VMEM((SLOTS, 8, full), F32),
            pltpu.VMEM((SLOTS, shard, width), F32),
            pltpu.VMEM((SLOTS, shard, width), F32),
            dma((SLOTS, 2)), dma((SLOTS, 2)), dma((SLOTS, 2)), dma((SLOTS, 2)),
            dma((SLOTS,)), dma((SLOTS,)), dma, dma,
            dma((SLOTS,)), dma((SLOTS,)), dma((SLOTS,)), dma((SLOTS,)),
            dma((SLOTS,)), dma((SLOTS,)),
        ],
        compiler_params=pltpu.CompilerParams(
            collective_id=0, has_side_effects=True, vmem_limit_bytes=60 * 1024 * 1024
        ),
    )(teacher, student)


def solution(mesh):
    return jax.shard_map(
        on_device,
        mesh=mesh,
        in_specs=(P(("row", "col"), None), P(("row", "col"), None)),
        out_specs=P(("row", "col"), None),
        check_vma=False,
    )
```

time: 509 us -> 114 us (0.22)
  waiting for transfers between devices: 320 us -> 0 us
  Pallas kernels: 0 us -> 111 us
  blocking collectives: 78.5 us -> 0 us
  matrix products: 70.5 us -> 0 us
  other arithmetic: 22.5 us -> 0 us
  between operations: 13.6 us -> 0.01 us
    all_gather x4 -> x0, waiting for transfers between devices: 180 us -> none  [the longest x1 54 us: on_device(): lax.all_gather(student, 'col', axis=0, tiled=True)]
    reduce_scatter x2 -> x0, waiting for transfers between devices: 137 us -> none  [the longest x1 71.8 us: on_device(): lax.psum_scatter(right_term(gtile, rows_s), 'row', scatter_dimension=0, t...]
    pallas_call x0 -> x1, Pallas kernels: none -> 111 us  [on_device(): pl.pallas_call(kernel, out_shape=jax.ShapeDtypeStruct((shard, width), F32...]
    dot_general x10 -> x0, matrix products: 70.5 us -> none  [the longest x4 28.8 us: scores_pair(): lax.dot_general(block_t, cols_t, dims, preferred_element_type=jnp.float32)]
    pmax x1 -> x0, blocking collectives: 41.7 us -> none  [reduce_stats(): top_t, top_s = lax.pmax((local[0], local[2]), 'col')]
    psum x1 -> x0, blocking collectives: 36.8 us -> none  [reduce_stats(): lax.psum((local[1] * jnp.exp(local[0] - top_t), local[3] * jnp.exp(local[...]
    reduce_sum x2 -> x0, other arithmetic: 13.5 us -> none  [first_pass(): jnp.sum(jnp.exp(zs - top_s[:, None]), axis=1)]
  transfers between devices with their start and end apart: 6 -> 0, of which waited for: 6 -> 0; matrix products, arithmetic and copies ran while one was open for 2% -> 0% of each run, Pallas kernels for 0% -> 0%
where the time goes in v1:
time: 114 us; the launch traced here: 113 us
  Pallas kernels  111 us (97%)
  local copies, waits for them, and re-layouts  1.77 us (2%)
    pallas_call x1, Pallas kernels, on_device(): pl.pallas_call(kernel, out_shape=jax.ShapeDtypeStruct((shard, width), F32...  111 us

profile of v1, /device:TPU:0, one launch (start us, length us, event | category | flops | bytes accessed | tf_op | source)
XLA Modules:
  0.0 113.2 jit_solution(607618276870845125)
XLA Ops:
  0.0 111.5 %shard_map.28 = f32[192,512]{1,0:T(8,128)} custom-call(bf16[192,512]{1,0:T(8,128)(2,1)} %t_ref.1, bf16[192,512]{1,0:T(8,128)(2,1)} %s_ref.1), custom_call_target="tpu_custom_call" | custom-call | tf_op jit(solution)/shard_map/pallas_call | solution.py:312
  111.5 1.8 %copy.4 = f32[192,512]{1,0:T(8,128)} copy(f32[192,512]{1,0:T(8,128)} %shard_map.28) | data formatting | bytes 786432

commit v2 on v1

v2 whole, which is shorter than its diff:
```python
import functools
import math

import jax
import jax.numpy as jnp
from jax import lax
from jax.experimental import pallas as pl
from jax.experimental.pallas import tpu as pltpu
from jax.sharding import PartitionSpec as P

F32 = jnp.float32
BF16 = jnp.bfloat16
MESH = pl.DeviceIdType.MESH
SIDE = 4

OFFSETS = (
    (0, 0, 0), (3, 0, 0), (0, 0, 1), (1, 0, 0), (0, 3, 3), (3, 1, 0),
    (1, 0, 1), (0, 2, 3), (3, 2, 0), (3, 1, 3), (1, 0, 2),
)
PARENT = (None, 0, 0, 0, 0, 1, 2, 4, 5, 5, 6)
SLOTS = len(OFFSETS)
CHILDREN = tuple(tuple(q for q in range(SLOTS) if PARENT[q] == p) for p in range(SLOTS))
LEVEL = []
for parent in PARENT:
    LEVEL.append(0 if parent is None else LEVEL[parent] + 1)
LEVELS = tuple(tuple(q for q in range(SLOTS) if LEVEL[q] == level) for level in range(4))

WORK = (
    (
        (2, 1, 0), (4, 3, 2),
        (1, 6, 5), (6, 5, 4), (7, 3, 0),
        (0, 10, 5), (10, 3, 1), (9, 7, 6), (10, 9, 8),
    ),
    (
        (0, 0, 1), (3, 2, 1), (4, 1, 0),
        (5, 4, 3), (2, 7, 5), (7, 6, 5),
        (8, 1, 0), (8, 6, 3), (9, 2, 1),
    ),
)
ITEMS = len(WORK[0])
STEPS = 2 * ITEMS
ROW_PIECES = 1
STUDENT_LATER = False
SUM_PIECES = 2


def minus(a, b):
    return tuple((p - q) % SIDE for p, q in zip(a, b))


def is_half(a, b):
    d = minus(OFFSETS[a], OFFSETS[b])
    return d == minus((0, 0, 0), d)


def check_work():
    found = [
        min(minus(OFFSETS[a], OFFSETS[b]), minus(OFFSETS[b], OFFSETS[a]))
        for work in WORK
        for a, b1, b2 in work
        for b in (b1, b2)
    ]
    assert len(found) == len(set(found)) == (SIDE**3 + 8) // 2


check_work()


def group_of(item, m):
    return max(max(LEVEL[q] for q in item), 1) - 1 + m


def sequence(core):
    steps = [
        (group_of(item, m), m, n) for n, item in enumerate(WORK[core]) for m in range(2)
    ]
    return tuple((m, n) for _, m, n in sorted(steps))


SEQUENCE = (sequence(0), sequence(1))
GROUP_START = tuple(
    min(
        min(s for s, (m, n) in enumerate(SEQUENCE[core]) if group_of(WORK[core][n], m) == g)
        for core in range(2)
    )
    for g in range(4)
)


def packed(item, m, n):
    a, b1, b2 = item
    return (
        a + b1 * 16 + b2 * 256 + int(is_half(a, b1)) * 4096 + int(is_half(a, b2)) * 8192
        + m * 16384 + n * 32768
    )


STEP_CODES = tuple(tuple(packed(WORK[c][n], m, n) for m, n in SEQUENCE[c]) for c in range(2))
ITEM_CODES = tuple(tuple(packed(item, 0, n) for n, item in enumerate(WORK[c])) for c in range(2))


def look_up(codes, core, at):
    value = jnp.int32(0)
    for n, (one, two) in enumerate(zip(*codes)):
        value = jnp.where(at == n, jnp.where(core == 0, jnp.int32(one), jnp.int32(two)), value)
    return value


def field(code, start, bits):
    return (code >> start) & ((1 << bits) - 1)


DONE = tuple(
    max(ITEMS - 1 - n for work in WORK for n, item in enumerate(work) if q in item)
    for q in range(SLOTS)
)
PASS_ON = {
    2: ((9, 0),), 3: ((8, 0),), 4: ((10, 0),), 5: ((9, 1), (7, 0)), 6: ((8, 1),), 7: ((5, 0), (10, 1)),
}
LAST = (
    (4, 0), (3, 0), (6, 0), (7, 1), (5, 1), (6, 1), (1, 0), (2, 0), (4, 1), (3, 1), (1, 1), (2, 1), (0, 0),
    (0, 1),
)
GATED = True


def kernel(
    t_ref, s_ref, o_ref, rows, z, acc, tile, diff, pen, stat, stat_out, stat_in, both, both_in, norm,
    half_in, part_in,
    tree_send, tree_recv, pair_send, pair_recv, stat_send, stat_recv, both_send, both_recv,
    norm_send, norm_recv, half_send, half_recv, part_send, part_recv,
):
    shard, width = t_ref.shape
    full = 2 * shard
    wide = 2 * full
    scale = 1.0 / (0.1 * math.sqrt(width))
    row = lax.axis_index("row")
    col = lax.axis_index("col")
    core = row & 1
    other = 1 - core
    x, y, zz = col & 3, (row >> 1) & 3, ((col >> 2) << 1) + (row >> 3)
    places = {}

    def device(d, sign=1):
        d = tuple((sign * q) % SIDE for q in d)
        if d not in places:
            to = [(p + q) & 3 if q else p for p, q in zip((x, y, zz), d)]
            places[d] = (((to[2] & 1) << 3) + (to[1] << 1) + core, ((to[2] >> 1) << 2) + to[0])
        return places[d]

    sibling = (row ^ 1, col)

    def edge(q):
        return minus(OFFSETS[q], OFFSETS[PARENT[q]])

    partners = set()
    for q in range(1, SLOTS):
        for d in (OFFSETS[q], edge(q)):
            partners.add(d)
            partners.add(minus((0, 0, 0), d))
    partners = sorted(partners)

    barrier = pltpu.get_barrier_semaphore()
    for d in partners:
        pl.semaphore_signal(barrier, inc=1, device_id=device(d), device_id_type=MESH)
    pl.semaphore_signal(barrier, inc=1, device_id=sibling, device_id_type=MESH)
    rows[0, 0, core] = t_ref[...]
    rows[0, 1, core] = s_ref[...]

    def remote(src, dst, send, recv, to):
        return pltpu.make_async_remote_copy(
            src_ref=src, dst_ref=dst, send_sem=send, recv_sem=recv, device_id=to, device_id_type=MESH
        )

    def piece(q, m, c):
        size = shard // ROW_PIECES
        return rows.at[q, m, core, pl.ds(c * size, size)]

    def tree(q, m, c):
        return remote(
            piece(PARENT[q], m, c), piece(q, m, c), tree_send.at[q, m, c], tree_recv.at[q, m, c],
            device(edge(q), -1),
        )

    def across(q, m, c):
        return remote(
            piece(q, m, c), piece(q, m, c), pair_send.at[q, m, c], pair_recv.at[q, m, c], sibling
        )

    def take_up(level, m):
        for c in range(ROW_PIECES):
            for q in LEVELS[level]:
                if q:
                    tree(q, m, c).wait_recv()
                for child in CHILDREN[q]:
                    tree(child, m, c).start()
                across(q, m, c).start()

    def arrive(level, m):
        for c in range(ROW_PIECES):
            for q in LEVELS[level]:
                across(q, m, c).wait_recv()

    def open_group(g):
        if g + 1 < len(LEVELS):
            take_up(g + 1, 0)
        if g or STUDENT_LATER:
            take_up(g, 1)
        if g == 0:
            arrive(0, 0)
        if g == 1:
            arrive(0, 1)
        if g + 1 < len(LEVELS):
            arrive(g + 1, 0)
        if g:
            arrive(g, 1)

    acc[...] = jnp.zeros_like(acc)
    for m in range(2):
        stat[:, m, 0:1, :] = jnp.full((SLOTS, 1, full), -1e30, F32)
        stat[:, m, 1:2, :] = jnp.zeros((SLOTS, 1, full), F32)
    pen[...] = jnp.where(
        lax.broadcasted_iota(jnp.int32, (128, 128), 0) == lax.broadcasted_iota(jnp.int32, (128, 128), 1),
        F32(-1e30), F32(0.0),
    )
    pl.semaphore_wait(barrier, len(partners) + 1)
    take_up(0, 0)
    if not STUDENT_LATER:
        take_up(0, 1)

    def block(q, m):
        return rows[q, m].reshape(full, width)

    def two(b1, b2, m):
        return jnp.concatenate([block(b1, m), block(b2, m)], axis=0)

    def ends(code):
        return field(code, 0, 4), field(code, 4, 4), field(code, 8, 4)

    def scores(code, par):
        a, b1, b2 = ends(code)
        m = field(code, 14, 1)
        less = [jnp.full((1, full), field(code, bit, 1).astype(F32)) for bit in (12, 13)]
        tile[par] = lax.dot_general(
            block(a, m), two(b1, b2, m), (((1,), (1,)), ((), ())), preferred_element_type=F32
        ) * (scale * math.log2(math.e)) - jnp.concatenate(less, axis=1)
        own = (a == b1).astype(F32)
        for k in range(0, full, 128):
            tile[par, k : k + 128, k : k + 128] += pen[...] * own

    def merge(ref, top, total):
        old = ref[0:1, :]
        new = jnp.maximum(old, top)
        ref[1:2, :] = ref[1:2, :] * jnp.exp2(old - new) + total * jnp.exp2(top - new)
        ref[0:1, :] = new

    def lanes(value):
        return [value[:, j : j + 128] for j in range(0, wide, 128)]

    def statistics(code, par):
        a, b1, b2 = ends(code)
        m = field(code, 14, 1)
        at = m * ITEMS + field(code, 15, 4)
        right, down = [], None
        for k in range(0, full, 128):
            score = tile[par, k : k + 128, :]
            z[at, k : k + 128, :] = score
            most = functools.reduce(jnp.maximum, lanes(score))
            right.append(jnp.max(jnp.transpose(most), axis=0, keepdims=True))
            most = jnp.max(score.reshape(16, 8, wide), axis=0)
            down = most if down is None else jnp.maximum(down, most)
        down = jnp.max(down, axis=0, keepdims=True)
        right = jnp.concatenate(right, axis=1)
        column = jnp.transpose(jnp.broadcast_to(right, (128, full)))
        right_sum, down_sum = [], None
        for k in range(0, full, 128):
            score = tile[par, k : k + 128, :]
            across_ = sum(jnp.exp2(part - column[k : k + 128]) for part in lanes(score))
            right_sum.append(jnp.sum(jnp.transpose(across_), axis=0, keepdims=True))
            below = jnp.sum(jnp.exp2(score - down).reshape(16, 8, wide), axis=0)
            down_sum = below if down_sum is None else down_sum + below
        down_sum = jnp.sum(down_sum, axis=0, keepdims=True)
        merge(stat.at[a, m], right, jnp.concatenate(right_sum, axis=1))
        merge(stat.at[b1, m], down[:, :full], down_sum[:, :full])
        merge(stat.at[b2, m], down[:, full:], down_sum[:, full:])

    open_group(0)
    first = look_up(STEP_CODES, core, 0)
    scores(first, 0)

    def first_pass(h, code):
        for par in range(2):
            for g in range(1, 4):
                if (GROUP_START[g] - 1) % 2 == par:
                    @pl.when(h == (GROUP_START[g] - 1) // 2)
                    def _(g=g):
                        open_group(g)
            later = look_up(STEP_CODES, core, jnp.minimum(2 * h + par + 1, STEPS - 1))
            scores(later, 1 - par)
            statistics(code, par)
            code = later
        return code

    lax.fori_loop(0, STEPS // 2, first_pass, first)

    def stat_copy(q):
        return remote(
            stat_out.at[q], stat_in.at[q], stat_send.at[q], stat_recv.at[q], device(OFFSETS[q])
        )

    def norm_copy(q):
        return remote(
            norm.at[0], norm.at[q], norm_send.at[q], norm_recv.at[q], device(OFFSETS[q], -1)
        )

    for q in range(1, SLOTS):
        for m in range(2):
            stat_out[q, 2 * m : 2 * m + 2, :] = stat[q, m, 0:2, :]
        stat_copy(q).start()
    for q in range(1, SLOTS):
        stat_copy(q).wait_recv()
    for m in range(2):
        tops = [stat[0, m, 0:1, :]] + [stat_in[q, 2 * m : 2 * m + 1, :] for q in range(1, SLOTS)]
        sums = [stat[0, m, 1:2, :]] + [stat_in[q, 2 * m + 1 : 2 * m + 2, :] for q in range(1, SLOTS)]
        top = functools.reduce(jnp.maximum, tops)
        both[2 * m : 2 * m + 1, :] = top
        both[2 * m + 1 : 2 * m + 2, :] = sum(s * jnp.exp2(t - top) for t, s in zip(tops, sums))
    both_copy = remote(both, both_in, both_send, both_recv, sibling)
    both_copy.start()
    both_copy.wait()
    for m in range(2):
        one, two_ = both[2 * m : 2 * m + 1, :], both_in[2 * m : 2 * m + 1, :]
        top = jnp.maximum(one, two_)
        norm[0, m : m + 1, :] = top + jnp.log2(
            both[2 * m + 1 : 2 * m + 2, :] * jnp.exp2(one - top)
            + both_in[2 * m + 1 : 2 * m + 2, :] * jnp.exp2(two_ - top)
        )
    for q in range(1, SLOTS):
        norm_copy(q).start()
    for q in range(1, SLOTS):
        norm_copy(q).wait_recv()

    def half_copy(q):
        return remote(acc.at[q, other], half_in.at[q], half_send.at[q], half_recv.at[q], sibling)

    def part_copy(q, c):
        size = shard // SUM_PIECES
        return remote(
            acc.at[q, core, pl.ds(c * size, size)], part_in.at[q, pl.ds(c * size, size)],
            part_send.at[q, c], part_recv.at[q, c], device(edge(q)),
        )

    def pass_on(q, c):
        if c == 0:
            half_copy(q).wait_recv()
        elif q and GATED:
            part_copy(q, c - 1).wait_send()
        size = shard // SUM_PIECES
        at = pl.ds(c * size, size)
        total = acc[q, core, at] + half_in[q, at]
        for child in CHILDREN[q]:
            part_copy(child, c).wait_recv()
            total = total + part_in[child, at]
        if q:
            acc[q, core, at] = total
            part_copy(q, c).start()
        else:
            o_ref[at] = scale * total

    def column_of(line):
        return jnp.concatenate([jnp.transpose(jnp.broadcast_to(line, (128, full)))] * (wide // 128), axis=1)

    def differences(code, par):
        a, b1, b2 = ends(code)
        n = field(code, 15, 4)
        left = [column_of(norm[a, m : m + 1, :]) for m in range(2)]
        top = [
            jnp.concatenate([norm[b1, m : m + 1, :], norm[b2, m : m + 1, :]], axis=1) for m in range(2)
        ]
        zt, zs = z[n], z[ITEMS + n]
        diff[par, 0] = (jnp.exp2(zs - left[1]) - jnp.exp2(zt - left[0])).astype(BF16)
        diff[par, 1] = (jnp.exp2(zs - top[1]) - jnp.exp2(zt - top[0])).astype(BF16)

    def products(code, par):
        a, b1, b2 = ends(code)
        by_row, by_col = diff[par, 0], diff[par, 1]
        sa, sb = block(a, 1), two(b1, b2, 1)
        forward = jnp.dot(
            jnp.concatenate([by_row, by_col], axis=1), jnp.concatenate([sb, sb], axis=0),
            preferred_element_type=F32,
        )
        acc[a] = acc[a] + forward.reshape(2, shard, width)
        backward = lax.dot_general(
            jnp.concatenate([by_row, by_col], axis=0), jnp.concatenate([sa, sa], axis=0),
            (((0,), (0,)), ((), ())), preferred_element_type=F32,
        )
        acc[b1] = acc[b1] + backward[:full].reshape(2, shard, width)
        acc[b2] = acc[b2] + backward[full:].reshape(2, shard, width)

    def after(step):
        for q in reversed(range(SLOTS)):
            if DONE[q] == step:
                half_copy(q).start()
        for q, c in PASS_ON.get(step, ()):
            pass_on(q, c)

    first = look_up(ITEM_CODES, core, ITEMS - 1)
    differences(first, 0)

    def second_pass(h, code):
        for par in range(2):
            later = look_up(ITEM_CODES, core, ITEMS - 2 - (2 * h + par))
            differences(later, 1 - par)
            products(code, par)
            code = later
            for step in range(par, ITEMS - 1, 2):
                if step in DONE or step in PASS_ON:
                    @pl.when(h == step // 2)
                    def _(step=step):
                        after(step)
        return code

    last = lax.fori_loop(0, (ITEMS - 1) // 2, second_pass, first)
    products(last, 0)
    after(ITEMS - 1)
    for q, c in LAST:
        pass_on(q, c)

    for q in range(SLOTS):
        for m in range(2):
            for c in range(ROW_PIECES):
                if q:
                    tree(q, m, c).wait_send()
                across(q, m, c).wait_send()
        half_copy(q).wait_send()
        if q:
            stat_copy(q).wait_send()
            norm_copy(q).wait_send()
            for c in range(SUM_PIECES - 1 if GATED else 0, SUM_PIECES):
                part_copy(q, c).wait_send()


def on_device(teacher, student):
    shard, width = teacher.shape
    full = 2 * shard
    dma = pltpu.SemaphoreType.DMA
    return pl.pallas_call(
        kernel,
        out_shape=jax.ShapeDtypeStruct((shard, width), F32),
        in_specs=[pl.BlockSpec(memory_space=pltpu.VMEM)] * 2,
        out_specs=pl.BlockSpec(memory_space=pltpu.VMEM),
        scratch_shapes=[
            pltpu.VMEM((SLOTS, 2, 2, shard, width), BF16),
            pltpu.VMEM((STEPS, full, 2 * full), F32),
            pltpu.VMEM((SLOTS, 2, shard, width), F32),
            pltpu.VMEM((2, full, 2 * full), F32),
            pltpu.VMEM((2, 2, full, 2 * full), BF16),
            pltpu.VMEM((128, 128), F32),
            pltpu.VMEM((SLOTS, 2, 8, full), F32),
            pltpu.VMEM((SLOTS, 4, full), F32),
            pltpu.VMEM((SLOTS, 4, full), F32),
            pltpu.VMEM((4, full), F32),
            pltpu.VMEM((4, full), F32),
            pltpu.VMEM((SLOTS, 2, full), F32),
            pltpu.VMEM((SLOTS, shard, width), F32),
            pltpu.VMEM((SLOTS, shard, width), F32),
            dma((SLOTS, 2, ROW_PIECES)), dma((SLOTS, 2, ROW_PIECES)),
            dma((SLOTS, 2, ROW_PIECES)), dma((SLOTS, 2, ROW_PIECES)),
            dma((SLOTS,)), dma((SLOTS,)), dma, dma,
            dma((SLOTS,)), dma((SLOTS,)), dma((SLOTS,)), dma((SLOTS,)),
            dma((SLOTS, SUM_PIECES)), dma((SLOTS, SUM_PIECES)),
        ],
        compiler_params=pltpu.CompilerParams(
            collective_id=0, has_side_effects=True, vmem_limit_bytes=62 * 1024 * 1024
        ),
    )(teacher, student)


def solution(mesh):
    return jax.shard_map(
        on_device,
        mesh=mesh,
        in_specs=(P(("row", "col"), None), P(("row", "col"), None)),
        out_specs=P(("row", "col"), None),
        check_vma=False,
    )
```

time: 114 us -> 96.4 us (0.85)
  Pallas kernels: 111 us -> 94.4 us
    pallas_call x1, Pallas kernels: 111 us -> 94.4 us  [on_device(): pl.pallas_call(kernel, out_shape=jax.ShapeDtypeStruct((shard, width), F32...]
where the time goes in v2:
time: 96.4 us; the launch traced here: 96.2 us
  Pallas kernels  94.4 us (98%)
  local copies, waits for them, and re-layouts  1.77 us (2%)
    pallas_call x1, Pallas kernels, on_device(): pl.pallas_call(kernel, out_shape=jax.ShapeDtypeStruct((shard, width), F32...  94.4 us

profile of v2, /device:TPU:0, one launch (start us, length us, event | category | flops | bytes accessed | tf_op | source)
XLA Modules:
  0.0 96.2 jit_solution(14315278620469599183)
XLA Ops:
  0.0 94.4 %shard_map.28 = f32[192,512]{1,0:T(8,128)} custom-call(bf16[192,512]{1,0:T(8,128)(2,1)} %t_ref.1, bf16[192,512]{1,0:T(8,128)(2,1)} %s_ref.1), custom_call_target="tpu_custom_call" | custom-call | tf_op jit(solution)/shard_map/pallas_call | solution.py:447
  94.4 1.8 %copy.4 = f32[192,512]{1,0:T(8,128)} copy(f32[192,512]{1,0:T(8,128)} %shard_map.28) | data formatting | bytes 786432

commit v3 on v2

--- a/solution.py
+++ b/solution.py
@@ -29,18 +29,17 @@
     (
         (2, 1, 0), (4, 3, 2),
         (1, 6, 5), (6, 5, 4), (7, 3, 0),
-        (0, 10, 5), (10, 3, 1), (9, 7, 6), (10, 9, 8),
+        (9, 7, 6), (0, 10, 5), (10, 3, 1), (10, 9, 8),
     ),
     (
         (0, 0, 1), (3, 2, 1), (4, 1, 0),
         (5, 4, 3), (2, 7, 5), (7, 6, 5),
-        (8, 1, 0), (8, 6, 3), (9, 2, 1),
+        (9, 2, 1), (8, 1, 0), (8, 6, 3),
     ),
 )
 ITEMS = len(WORK[0])
 STEPS = 2 * ITEMS
 ROW_PIECES = 1
-STUDENT_LATER = False
 SUM_PIECES = 2
 
 
@@ -71,9 +70,7 @@
 
 
 def sequence(core):
-    steps = [
-        (group_of(item, m), m, n) for n, item in enumerate(WORK[core]) for m in range(2)
-    ]
+    steps = [(group_of(item, m), m, n) for n, item in enumerate(WORK[core]) for m in range(2)]
     return tuple((m, n) for _, m, n in sorted(steps))
 
 
@@ -85,6 +82,9 @@
     )
     for g in range(4)
 )
+TAKEN = {-1: ((0, 0), (0, 1), (1, 0), (1, 1), (2, 0)), 0: ((2, 1), (3, 0)), 6: ((3, 1),)}
+HANDED = {-1: ((0, 0), (1, 0)), 0: ((2, 0), (0, 1), (1, 1)), 6: ((3, 0),), 10: ((2, 1),), 12: ((3, 1),)}
+assert GROUP_START == (0, 2, 7, 14)
 
 
 def packed(item, m, n):
@@ -114,14 +114,19 @@
     max(ITEMS - 1 - n for work in WORK for n, item in enumerate(work) if q in item)
     for q in range(SLOTS)
 )
+GOES_TO = {(q, c): PARENT[q] for q in range(1, SLOTS) for c in range(SUM_PIECES)}
+GOES_TO[5, 1] = 0
+GOES_TO[6, 0] = 3
 PASS_ON = {
-    2: ((9, 0),), 3: ((8, 0),), 4: ((10, 0),), 5: ((9, 1), (7, 0)), 6: ((8, 1),), 7: ((5, 0), (10, 1)),
+    3: ((8, 0), (10, 0)), 4: ((9, 0),), 5: ((8, 1), (10, 1), (7, 0)), 6: ((9, 1),), 7: ((7, 1),),
 }
 LAST = (
-    (4, 0), (3, 0), (6, 0), (7, 1), (5, 1), (6, 1), (1, 0), (2, 0), (4, 1), (3, 1), (1, 1), (2, 1), (0, 0),
-    (0, 1),
+    (6, 0), (4, 0), (3, 1), (5, 0), (1, 1), (2, 0), (6, 1), (4, 1), (5, 1), (3, 0), (1, 0), (2, 1), (0, 0), (0, 1),
 )
-GATED = True
+ORDER = tuple(piece for step in sorted(PASS_ON) for piece in PASS_ON[step]) + LAST
+FIRST = tuple(next(piece for piece in ORDER if piece[0] == q) for q in range(SLOTS))
+SECOND = tuple(next(piece for piece in ORDER[::-1] if piece[0] == q) for q in range(SLOTS))
+assert len(set(ORDER)) == len(ORDER) == SLOTS * SUM_PIECES == 2 * SLOTS
 
 
 def kernel(
@@ -153,9 +158,12 @@
     def edge(q):
         return minus(OFFSETS[q], OFFSETS[PARENT[q]])
 
+    def sum_edge(q, c):
+        return minus(OFFSETS[q], OFFSETS[GOES_TO[q, c]])
+
     partners = set()
     for q in range(1, SLOTS):
-        for d in (OFFSETS[q], edge(q)):
+        for d in [OFFSETS[q], edge(q)] + [sum_edge(q, c) for c in range(SUM_PIECES)]:
             partners.add(d)
             partners.add(minus((0, 0, 0), d))
     partners = sorted(partners)
@@ -183,37 +191,31 @@
         )
 
     def across(q, m, c):
-        return remote(
-            piece(q, m, c), piece(q, m, c), pair_send.at[q, m, c], pair_recv.at[q, m, c], sibling
-        )
-
-    def take_up(level, m):
-        for c in range(ROW_PIECES):
-            for q in LEVELS[level]:
-                if q:
-                    tree(q, m, c).wait_recv()
-                for child in CHILDREN[q]:
-                    tree(child, m, c).start()
-                across(q, m, c).start()
+        part = piece(q, m, c)
+        return remote(part, part, pair_send.at[q, m, c], pair_recv.at[q, m, c], sibling)
+
+    def take_up(level, n):
+        m, c = n // ROW_PIECES, n % ROW_PIECES
+        if level == 0 and n:
+            for child in CHILDREN[0]:
+                tree(child, (n - 1) // ROW_PIECES, (n - 1) % ROW_PIECES).wait_send()
+        for q in LEVELS[level]:
+            if q:
+                tree(q, m, c).wait_recv()
+            for child in CHILDREN[q]:
+                tree(child, m, c).start()
+            across(q, m, c).start()
 
     def arrive(level, m):
-        for c in range(ROW_PIECES):
-            for q in LEVELS[level]:
+        for q in LEVELS[level]:
+            for c in range(ROW_PIECES):
                 across(q, m, c).wait_recv()
 
-    def open_group(g):
-        if g + 1 < len(LEVELS):
-            take_up(g + 1, 0)
-        if g or STUDENT_LATER:
-            take_up(g, 1)
-        if g == 0:
-            arrive(0, 0)
-        if g == 1:
-            arrive(0, 1)
-        if g + 1 < len(LEVELS):
-            arrive(g + 1, 0)
-        if g:
-            arrive(g, 1)
+    def before(step):
+        for level, n in TAKEN.get(step, ()):
+            take_up(level, n)
+        for level, m in HANDED.get(step, ()):
+            arrive(level, m)
 
     acc[...] = jnp.zeros_like(acc)
     for m in range(2):
@@ -224,9 +226,6 @@
         F32(-1e30), F32(0.0),
     )
     pl.semaphore_wait(barrier, len(partners) + 1)
-    take_up(0, 0)
-    if not STUDENT_LATER:
-        take_up(0, 1)
 
     def block(q, m):
         return rows[q, m].reshape(full, width)
@@ -284,17 +283,17 @@
         merge(stat.at[b1, m], down[:, :full], down_sum[:, :full])
         merge(stat.at[b2, m], down[:, full:], down_sum[:, full:])
 
-    open_group(0)
+    before(-1)
     first = look_up(STEP_CODES, core, 0)
     scores(first, 0)
 
     def first_pass(h, code):
+        for step in sorted(set(TAKEN) | set(HANDED)):
+            if step >= 0:
+                @pl.when(2 * h == step)
+                def _(step=step):
+                    before(step)
         for par in range(2):
-            for g in range(1, 4):
-                if (GROUP_START[g] - 1) % 2 == par:
-                    @pl.when(h == (GROUP_START[g] - 1) // 2)
-                    def _(g=g):
-                        open_group(g)
             later = look_up(STEP_CODES, core, jnp.minimum(2 * h + par + 1, STEPS - 1))
             scores(later, 1 - par)
             statistics(code, par)
@@ -347,20 +346,21 @@
         size = shard // SUM_PIECES
         return remote(
             acc.at[q, core, pl.ds(c * size, size)], part_in.at[q, pl.ds(c * size, size)],
-            part_send.at[q, c], part_recv.at[q, c], device(edge(q)),
+            part_send.at[q, c], part_recv.at[q, c], device(sum_edge(q, c)),
         )
 
     def pass_on(q, c):
-        if c == 0:
+        if (q, c) in FIRST:
             half_copy(q).wait_recv()
-        elif q and GATED:
-            part_copy(q, c - 1).wait_send()
+        elif q:
+            part_copy(q, 1 - c).wait_send()
         size = shard // SUM_PIECES
         at = pl.ds(c * size, size)
         total = acc[q, core, at] + half_in[q, at]
-        for child in CHILDREN[q]:
-            part_copy(child, c).wait_recv()
-            total = total + part_in[child, at]
+        for child in range(1, SLOTS):
+            if GOES_TO[child, c] == q:
+                part_copy(child, c).wait_recv()
+                total = total + part_in[child, at]
         if q:
             acc[q, core, at] = total
             part_copy(q, c).start()
@@ -429,15 +429,14 @@
     for q in range(SLOTS):
         for m in range(2):
             for c in range(ROW_PIECES):
-                if q:
+                if q and (PARENT[q] or m == 1 and c == ROW_PIECES - 1):
                     tree(q, m, c).wait_send()
                 across(q, m, c).wait_send()
         half_copy(q).wait_send()
         if q:
             stat_copy(q).wait_send()
             norm_copy(q).wait_send()
-            for c in range(SUM_PIECES - 1 if GATED else 0, SUM_PIECES):
-                part_copy(q, c).wait_send()
+            part_copy(*SECOND[q]).wait_send()
 
 
 def on_device(teacher, student):

time: 96.4 us -> 94.2 us (0.977)
  Pallas kernels: 94.4 us -> 92.2 us
    pallas_call x1, Pallas kernels: 94.4 us -> 92.2 us  [on_device(): pl.pallas_call(kernel, out_shape=jax.ShapeDtypeStruct((shard, width), F32...]
where the time goes in v3:
time: 94.2 us; the launch traced here: 94 us
  Pallas kernels  92.2 us (98%)
  local copies, waits for them, and re-layouts  1.77 us (2%)
    pallas_call x1, Pallas kernels, on_device(): pl.pallas_call(kernel, out_shape=jax.ShapeDtypeStruct((shard, width), F32...  92.2 us

profile of v3, /device:TPU:0, one launch (start us, length us, event | category | flops | bytes accessed | tf_op | source)
XLA Modules:
  0.0 94.0 jit_solution(2355943215639789066)
XLA Ops:
  0.0 92.2 %shard_map.28 = f32[192,512]{1,0:T(8,128)} custom-call(bf16[192,512]{1,0:T(8,128)(2,1)} %t_ref.1, bf16[192,512]{1,0:T(8,128)(2,1)} %s_ref.1), custom_call_target="tpu_custom_call" | custom-call | tf_op jit(solution)/shard_map/pallas_call | solution.py:446
  92.2 1.8 %copy.4 = f32[192,512]{1,0:T(8,128)} copy(f32[192,512]{1,0:T(8,128)} %shard_map.28) | data formatting | bytes 786432

commit v4 on v3

--- a/solution.py
+++ b/solution.py
@@ -82,8 +82,8 @@
     )
     for g in range(4)
 )
-TAKEN = {-1: ((0, 0), (0, 1), (1, 0), (1, 1), (2, 0)), 0: ((2, 1), (3, 0)), 6: ((3, 1),)}
-HANDED = {-1: ((0, 0), (1, 0)), 0: ((2, 0), (0, 1), (1, 1)), 6: ((3, 0),), 10: ((2, 1),), 12: ((3, 1),)}
+TAKEN = {-1: ((0, 0), (0, 1), (1, 0), (1, 1), (2, 0)), 1: ((2, 1), (3, 0)), 9: ((3, 1),)}
+HANDED = {-1: ((0, 0), (1, 0)), 1: ((2, 0), (0, 1), (1, 1)), 5: ((3, 0),), 9: ((2, 1),), 13: ((3, 1),)}
 assert GROUP_START == (0, 2, 7, 14)
 
 
@@ -109,6 +109,8 @@
 def field(code, start, bits):
     return (code >> start) & ((1 << bits) - 1)
 
+
+FAR_FIRST = tuple(sorted(range(1, SLOTS), key=lambda q: -sum(min(d, SIDE - d) for d in OFFSETS[q])))
 
 DONE = tuple(
     max(ITEMS - 1 - n for work in WORK for n, item in enumerate(work) if q in item)
@@ -123,6 +125,7 @@
 LAST = (
     (6, 0), (4, 0), (3, 1), (5, 0), (1, 1), (2, 0), (6, 1), (4, 1), (5, 1), (3, 0), (1, 0), (2, 1), (0, 0), (0, 1),
 )
+OWN_HALF_AFTER = (2, 0)
 ORDER = tuple(piece for step in sorted(PASS_ON) for piece in PASS_ON[step]) + LAST
 FIRST = tuple(next(piece for piece in ORDER if piece[0] == q) for q in range(SLOTS))
 SECOND = tuple(next(piece for piece in ORDER[::-1] if piece[0] == q) for q in range(SLOTS))
@@ -284,23 +287,25 @@
         merge(stat.at[b2, m], down[:, full:], down_sum[:, full:])
 
     before(-1)
-    first = look_up(STEP_CODES, core, 0)
+    first, second = look_up(STEP_CODES, core, 0), look_up(STEP_CODES, core, 1)
     scores(first, 0)
+    scores(second, 1)
+    statistics(first, 0)
 
     def first_pass(h, code):
         for step in sorted(set(TAKEN) | set(HANDED)):
             if step >= 0:
-                @pl.when(2 * h == step)
+                @pl.when(2 * h + 1 == step)
                 def _(step=step):
                     before(step)
-        for par in range(2):
-            later = look_up(STEP_CODES, core, jnp.minimum(2 * h + par + 1, STEPS - 1))
+        for par in (1, 0):
+            later = look_up(STEP_CODES, core, 2 * h + 3 - par)
             scores(later, 1 - par)
             statistics(code, par)
             code = later
         return code
 
-    lax.fori_loop(0, STEPS // 2, first_pass, first)
+    statistics(lax.fori_loop(0, STEPS // 2 - 1, first_pass, second), 1)
 
     def stat_copy(q):
         return remote(
@@ -312,7 +317,7 @@
             norm.at[0], norm.at[q], norm_send.at[q], norm_recv.at[q], device(OFFSETS[q], -1)
         )
 
-    for q in range(1, SLOTS):
+    for q in FAR_FIRST:
         for m in range(2):
             stat_out[q, 2 * m : 2 * m + 2, :] = stat[q, m, 0:2, :]
         stat_copy(q).start()
@@ -334,7 +339,7 @@
             both[2 * m + 1 : 2 * m + 2, :] * jnp.exp2(one - top)
             + both_in[2 * m + 1 : 2 * m + 2, :] * jnp.exp2(two_ - top)
         )
-    for q in range(1, SLOTS):
+    for q in FAR_FIRST:
         norm_copy(q).start()
     for q in range(1, SLOTS):
         norm_copy(q).wait_recv()
@@ -399,7 +404,7 @@
 
     def after(step):
         for q in reversed(range(SLOTS)):
-            if DONE[q] == step:
+            if q and DONE[q] == step:
                 half_copy(q).start()
         for q, c in PASS_ON.get(step, ()):
             pass_on(q, c)
@@ -425,6 +430,8 @@
     after(ITEMS - 1)
     for q, c in LAST:
         pass_on(q, c)
+        if (q, c) == OWN_HALF_AFTER:
+            half_copy(0).start()
 
     for q in range(SLOTS):
         for m in range(2):

time: 94.2 us -> 93.1 us (0.988)
  Pallas kernels: 92.2 us -> 91.2 us
    pallas_call x1, Pallas kernels: 92.2 us -> 91.2 us  [on_device(): pl.pallas_call(kernel, out_shape=jax.ShapeDtypeStruct((shard, width), F32...]
where the time goes in v4:
time: 93.1 us; the launch traced here: 93 us
  Pallas kernels  91.2 us (98%)
  local copies, waits for them, and re-layouts  1.77 us (2%)
    pallas_call x1, Pallas kernels, on_device(): pl.pallas_call(kernel, out_shape=jax.ShapeDtypeStruct((shard, width), F32...  91.2 us

profile of v4, /device:TPU:0, one launch (start us, length us, event | category | flops | bytes accessed | tf_op | source)
XLA Modules:
  0.0 93.0 jit_solution(17846226927119108887)
XLA Ops:
  0.0 91.2 %shard_map.28 = f32[192,512]{1,0:T(8,128)} custom-call(bf16[192,512]{1,0:T(8,128)(2,1)} %t_ref.1, bf16[192,512]{1,0:T(8,128)(2,1)} %s_ref.1), custom_call_target="tpu_custom_call" | custom-call | tf_op jit(solution)/shard_map/pallas_call | solution.py:453
  91.2 1.8 %copy.4 = f32[192,512]{1,0:T(8,128)} copy(f32[192,512]{1,0:T(8,128)} %shard_map.28) | data formatting | bytes 786432

commit v5 on v4

--- a/solution.py
+++ b/solution.py
@@ -82,7 +82,7 @@
     )
     for g in range(4)
 )
-TAKEN = {-1: ((0, 0), (0, 1), (1, 0), (1, 1), (2, 0)), 1: ((2, 1), (3, 0)), 9: ((3, 1),)}
+TAKEN = {-1: ((0, 1), (1, 0), (1, 1), (2, 0)), 1: ((2, 1), (3, 0)), 9: ((3, 1),)}
 HANDED = {-1: ((0, 0), (1, 0)), 1: ((2, 0), (0, 1), (1, 1)), 5: ((3, 0),), 9: ((2, 1),), 13: ((3, 1),)}
 assert GROUP_START == (0, 2, 7, 14)
 
@@ -220,6 +220,9 @@
         for level, m in HANDED.get(step, ()):
             arrive(level, m)
 
+    pl.semaphore_wait(barrier, len(partners) + 1)
+    take_up(0, 0)
+
     acc[...] = jnp.zeros_like(acc)
     for m in range(2):
         stat[:, m, 0:1, :] = jnp.full((SLOTS, 1, full), -1e30, F32)
@@ -228,7 +231,6 @@
         lax.broadcasted_iota(jnp.int32, (128, 128), 0) == lax.broadcasted_iota(jnp.int32, (128, 128), 1),
         F32(-1e30), F32(0.0),
     )
-    pl.semaphore_wait(barrier, len(partners) + 1)
 
     def block(q, m):
         return rows[q, m].reshape(full, width)
@@ -331,7 +333,7 @@
         both[2 * m + 1 : 2 * m + 2, :] = sum(s * jnp.exp2(t - top) for t, s in zip(tops, sums))
     both_copy = remote(both, both_in, both_send, both_recv, sibling)
     both_copy.start()
-    both_copy.wait()
+    both_copy.wait_recv()
     for m in range(2):
         one, two_ = both[2 * m : 2 * m + 1, :], both_in[2 * m : 2 * m + 1, :]
         top = jnp.maximum(one, two_)
@@ -433,6 +435,7 @@
         if (q, c) == OWN_HALF_AFTER:
             half_copy(0).start()
 
+    both_copy.wait_send()
     for q in range(SLOTS):
         for m in range(2):
             for c in range(ROW_PIECES):

time: 93.1 us -> 93 us (level)
  no operation moved by 1% of the time
where the time goes in v5:
time: 93 us; the launch traced here: 92.9 us
  Pallas kernels  91.1 us (98%)
  local copies, waits for them, and re-layouts  1.77 us (2%)
    pallas_call x1, Pallas kernels, on_device(): pl.pallas_call(kernel, out_shape=jax.ShapeDtypeStruct((shard, width), F32...  91.1 us

profile of v5, /device:TPU:0, one launch (start us, length us, event | category | flops | bytes accessed | tf_op | source)
XLA Modules:
  0.0 92.9 jit_solution(16818805832322416392)
XLA Ops:
  0.0 91.1 %shard_map.28 = f32[192,512]{1,0:T(8,128)} custom-call(bf16[192,512]{1,0:T(8,128)(2,1)} %t_ref.1, bf16[192,512]{1,0:T(8,128)(2,1)} %s_ref.1), custom_call_target="tpu_custom_call" | custom-call | tf_op jit(solution)/shard_map/pallas_call | solution.py:456
  91.1 1.8 %copy.4 = f32[192,512]{1,0:T(8,128)} copy(f32[192,512]{1,0:T(8,128)} %shard_map.28) | data formatting | bytes 786432

commit v6 on v5

--- a/solution.py
+++ b/solution.py
@@ -205,8 +205,9 @@
         for q in LEVELS[level]:
             if q:
                 tree(q, m, c).wait_recv()
-            for child in CHILDREN[q]:
+            for child in sorted(CHILDREN[q], key=lambda p: not CHILDREN[p]):
                 tree(child, m, c).start()
+        for q in LEVELS[level]:
             across(q, m, c).start()
 
     def arrive(level, m):

time: 93 us -> 93 us (level)
  no operation moved by 1% of the time
where the time goes in v6:
time: 93 us; the launch traced here: 92.9 us
  Pallas kernels  91.1 us (98%)
  local copies, waits for them, and re-layouts  1.77 us (2%)
    pallas_call x1, Pallas kernels, on_device(): pl.pallas_call(kernel, out_shape=jax.ShapeDtypeStruct((shard, width), F32...  91.1 us

profile of v6, /device:TPU:0, one launch (start us, length us, event | category | flops | bytes accessed | tf_op | source)
XLA Modules:
  0.0 92.9 jit_solution(14449959387354028905)
XLA Ops:
  0.0 91.1 %shard_map.28 = f32[192,512]{1,0:T(8,128)} custom-call(bf16[192,512]{1,0:T(8,128)(2,1)} %t_ref.1, bf16[192,512]{1,0:T(8,128)(2,1)} %s_ref.1), custom_call_target="tpu_custom_call" | custom-call | tf_op jit(solution)/shard_map/pallas_call | solution.py:457
  91.1 1.8 %copy.4 = f32[192,512]{1,0:T(8,128)} copy(f32[192,512]{1,0:T(8,128)} %shard_map.28) | data formatting | bytes 786432
